TPU v7x, 1024 devices: a whole 4x8x16 slice. The times are simulated.
1024 devices in a mesh: narrow: 16 (over x, y_lo), wide: 64 (over z, y_hi, core).
Axes of the slice: x: 4, y: 8 (y_hi: 2, y_lo: 4; y = y_hi * 4 + y_lo), z: 16, core: 2. Of those that a mesh axis runs over, the one named last changes fastest.
Arguments:
- amplitudes: float32 [16, 64, 2, 2, 256, 256], P('narrow', 'wide'), may hold values from -6 to 6
- first_gate: float32 [2, 256, 256], replicated, may hold values from -0.25 to 0.25
- second_gate: float32 [2, 256, 256], replicated, may hold values from -0.25 to 0.25
- swap_gates: float32 [2, 2, 256, 256], replicated, may hold values from -0.25 to 0.25
Outputs:
- final_state: float32 [16, 64, 2, 2, 256, 256], P('narrow', 'wide')
All inputs are finite; a program needn't handle non-finite values.
Results may differ from a plain program's by a relative error of at most 0.00007.
Values sent between devices are 32-bit elements; how exact they have to be, the bound alone decides.
A program may use at most 32 MiB of HBM per device.

v0:
```python
import jax
import jax.numpy as jnp
from jax import lax
from jax.sharding import PartitionSpec as P


def from_partner(block, axis, bit):
    count = lax.axis_size(axis)
    route = []
    for low in range(count):
        high = low | 1 << bit
        if high != low and high < count:
            route += [(low, high), (high, low)]
    return lax.ppermute(block, axis, route)


def mixing(matrix, values, form):
    return jnp.einsum(form, matrix, values, precision=lax.Precision.HIGHEST)


def turn_rows(gate, field):
    real = field[:, :, 0]
    imag = field[:, :, 1]
    form = "ij,nwcjb->nwcib"
    out_real = mixing(gate[0], real, form) - mixing(gate[1], imag, form)
    out_imag = mixing(gate[0], imag, form) + mixing(gate[1], real, form)
    return jnp.stack([out_real, out_imag], axis=2)


def turn_columns(gate, field):
    real = field[:, :, 0]
    imag = field[:, :, 1]
    form = "ij,nwcaj->nwcai"
    out_real = mixing(gate[0], real, form) - mixing(gate[1], imag, form)
    out_imag = mixing(gate[0], imag, form) + mixing(gate[1], real, form)
    return jnp.stack([out_real, out_imag], axis=2)


def half_swap(field, bit, pending):
    shape = field.shape
    halves = field.reshape(shape[0], shape[1], shape[2], shape[3], 2, shape[4] // 2, shape[5])
    upper = lax.axis_index("narrow") >> bit & 1 == 1
    lower_half = halves[:, :, :, :, 0]
    upper_half = halves[:, :, :, :, 1]
    outgoing = jnp.where(upper, lower_half, upper_half)
    kept = jnp.where(upper, upper_half, lower_half)
    if pending is not None:
        outgoing = turn_columns(pending, outgoing)
    incoming = from_partner(outgoing, "narrow", bit)
    if pending is not None:
        kept = turn_columns(pending, kept)
    new_lower = jnp.where(upper, incoming, kept)
    new_upper = jnp.where(upper, kept, incoming)
    return jnp.stack([new_lower, new_upper], axis=4).reshape(shape)


def shards(amplitudes, first_gate, second_gate, swap_gates):
    top_bit = lax.axis_size("narrow").bit_length() - 2
    state = turn_rows(first_gate, amplitudes)
    state = half_swap(state, 0, second_gate)
    state = turn_rows(swap_gates[0], state)
    state = half_swap(state, top_bit, None)
    last = swap_gates[1]
    state = turn_rows(last, state)
    final_state = lax.all_to_all(state, "wide", split_axis=5, concat_axis=5, tiled=True)
    return final_state


def solution(mesh):
    in_specs = (P("narrow", "wide", None, None, None, None), P(), P(), P())
    out_specs = P("narrow", "wide", None, None, None, None)
    return jax.shard_map(shards, mesh=mesh, in_specs=in_specs, out_specs=out_specs, check_vma=False)
```

profile of v0, /device:TPU:1, one launch (start us, length us, event | category | flops | bytes accessed | tf_op | source)
XLA Modules:
  0.0 132.2 jit_solution(1186137934898898007)
XLA Ops:
  0.0 1.8 %fusion.13 = f32[2,256,256]{1,2,0:T(8,128)S(1)} fusion(f32[1,1,2,2,256,256]{5,4,3,2,1,0:T(8,128)} %param.4, f32[2,256,256]{2,1,0:T(8,128)} %param.5), kind=kOutput, calls=%fused_computation.41 | convolution fusion | flops 402653184 | bytes 1310720 | tf_op jit(solution)/shard_map/ij,nwcjb->nwcib/dot_general | solution.py:18
  1.9 1.7 %fusion.17 = f32[2,256,256]{1,2,0:T(8,128)S(1)} fusion(f32[1,1,2,2,256,256]{5,4,3,2,1,0:T(8,128)S(1)} %copy-done.2, f32[2,256,256]{2,1,0:T(8,128)} %param.5), kind=kOutput, calls=%fused_computation.45 | convolution fusion | flops 402653184 | bytes 1310720 | tf_op jit(solution)/shard_map/ij,nwcjb->nwcib/dot_general | solution.py:18
  3.5 0.6 convolution_add_fusion.2
  4.2 0.6 convolution_subtract_fusion.2
  4.8 0.1 select_bitcast_fusion.2
  5.0 0.9 copy-done
  5.9 0.4 fusion.43
  6.3 0.4 fusion.45
  6.7 0.4 fusion.4
  7.1 0.4 fusion.5
  7.6 4.0 %collective-permute-start = (f32[1,1,2,2,128,256]{5,4,3,2,1,0:T(8,128)S(1)}, f32[1,1,2,2,128,256]{5,4,3,2,1,0:T(8,128)S(1)}, u32[]{:S(2)}, u32[]{:S(2)}) collective-permute-start(f32[1,1,2,2,128,256]{5,4,3,2,1,0:T(8,128)S(1)} %pad_maximum_fusion.5), channel_id=1, source_target_pairs={{0,64},{64,0},{128,192},{192,128},{256,320},{320,256},{384,448},{4... | collective-permute-start | bytes 1572872 | tf_op jit(solution)/shard_map/ppermute | solution.py:14
  11.6 0.4 fusion.39
  12.1 0.4 fusion.2
  12.5 0.4 fusion.41
  12.9 0.4 fusion.3
  13.3 4.9 %collective-permute-done = f32[1,1,2,2,128,256]{5,4,3,2,1,0:T(8,128)S(1)} collective-permute-done((f32[1,1,2,2,128,256]{5,4,3,2,1,0:T(8,128)S(1)}, f32[1,1,2,2,128,256]{5,4,3,2,1,0:T(8,128)S(1)}, u32[]{:S(2)}, u32[]{:S(2)}) %collective-permute-start) | collective-permute-done | bytes 524320 | tf_op jit(solution)/shard_map/ppermute | solution.py:14
  18.5 1.1 copy-done.1
  19.6 0.6 fusion.20
  20.2 0.6 fusion.19
  20.9 0.6 convolution_add_fusion.1
  21.5 0.6 convolution_subtract_fusion.1
  22.3 9.7 %collective-permute-start.1 = (f32[1,1,2,2,128,256]{5,4,3,2,1,0:T(8,128)S(1)}, f32[1,1,2,2,128,256]{5,4,3,2,1,0:T(8,128)S(1)}, u32[]{:S(2)}, u32[]{:S(2)}) collective-permute-start(f32[1,1,2,2,128,256]{5,4,3,2,1,0:T(8,128)S(1)} %fusion.10), channel_id=1, source_target_pairs={{0,512},{512,0},{64,576},{576,64},{128,640},{640,128},{192,704},{7... | collective-permute-start | bytes 1572872 | tf_op jit(solution)/shard_map/ppermute | solution.py:14
  32.0 6.4 %collective-permute-done.1 = f32[1,1,2,2,128,256]{5,4,3,2,1,0:T(8,128)S(1)} collective-permute-done((f32[1,1,2,2,128,256]{5,4,3,2,1,0:T(8,128)S(1)}, f32[1,1,2,2,128,256]{5,4,3,2,1,0:T(8,128)S(1)}, u32[]{:S(2)}, u32[]{:S(2)}) %collective-permute-start.1) | collective-permute-done | bytes 524320 | tf_op jit(solution)/shard_map/ppermute | solution.py:14
  38.6 0.6 copy.29
  39.2 0.8 reshape.215
  40.0 0.6 fusion.22
  40.6 0.6 fusion.21
  41.3 0.6 fusion
  41.9 0.6 fusion.1
  42.6 0.8 copy.30
  43.4 87.4 %all_to_all.5 = f32[1,1,2,2,256,256]{4,3,2,1,0,5:T(2,128)S(1)} all-to-all(f32[1,1,2,2,256,256]{4,3,2,1,0,5:T(2,128)S(1)} %copy.30), channel_id=1, replica_groups=mesh['narrow'=16,'wide'=64] {'wide'}, dimensions={5} | all-to-all | bytes 2097152 | tf_op jit(solution)/shard_map/all_to_all | solution.py:65
  130.8 1.4 %copy.31 = f32[1,1,2,2,256,256]{5,4,3,2,1,0:T(8,128)} copy(f32[1,1,2,2,256,256]{4,3,2,1,0,5:T(2,128)S(1)} %all_to_all.5) | data formatting | bytes 2097152 | tf_op jit(solution)/shard_map/all_to_all | solution.py:65
  (14 shorter events, 0.6 us)
Async XLA Ops:
  0.0 1.8 %copy-start.2 = (f32[1,1,2,2,256,256]{5,4,3,2,1,0:T(8,128)S(1)}, f32[1,1,2,2,256,256]{5,4,3,2,1,0:T(8,128)}, u32[]{:S(2)}) copy-start(f32[1,1,2,2,256,256]{5,4,3,2,1,0:T(8,128)} %param.4) | copy-start | bytes 3145732
  1.9 1.7 %copy-start.3 = (f32[2,256,256]{2,1,0:T(8,128)S(1)}, f32[2,256,256]{2,1,0:T(8,128)}, u32[]{:S(2)}) copy-start(f32[2,256,256]{2,1,0:T(8,128)} %param.5) | copy-start | bytes 1572868
  4.8 1.0 copy-start
  7.6 10.6 %collective-permute-start = (f32[1,1,2,2,128,256]{5,4,3,2,1,0:T(8,128)S(1)}, f32[1,1,2,2,128,256]{5,4,3,2,1,0:T(8,128)S(1)}, u32[]{:S(2)}, u32[]{:S(2)}) collective-permute-start(f32[1,1,2,2,128,256]{5,4,3,2,1,0:T(8,128)S(1)} %pad_maximum_fusion.5), channel_id=1, source_target_pairs={{0,64},{64,0},{128,192},{192,128},{256,320},{320,256},{384,448},{4... | collective-permute-start | bytes 1572872 | tf_op jit(solution)/shard_map/ppermute | solution.py:14
  18.4 1.2 copy-start.1
  22.3 16.1 %collective-permute-start.1 = (f32[1,1,2,2,128,256]{5,4,3,2,1,0:T(8,128)S(1)}, f32[1,1,2,2,128,256]{5,4,3,2,1,0:T(8,128)S(1)}, u32[]{:S(2)}, u32[]{:S(2)}) collective-permute-start(f32[1,1,2,2,128,256]{5,4,3,2,1,0:T(8,128)S(1)} %fusion.10), channel_id=1, source_target_pairs={{0,512},{512,0},{64,576},{576,64},{128,640},{640,128},{192,704},{7... | collective-permute-start | bytes 1572872 | tf_op jit(solution)/shard_map/ppermute | solution.py:14
where the time goes:
time: 132 us
  blocking collectives  87.4 us (66%)
  starting transfers between devices  13.8 us (10%)
  matrix products  13.1 us (10%)
  waiting for transfers between devices  11.2 us (8%)
  local copies, waits for them, and re-layouts  5.78 us (4%)
    all_to_all x1, blocking collectives, shards(): lax.all_to_all(state, 'wide', split_axis=5, concat_axis=5, tiled=True)  87.4 us
    ppermute x2, starting transfers between devices, from_partner(): return lax.ppermute(block, axis, route)  13.8 us
    dot_general x20, matrix products, mixing(): return jnp.einsum(form, matrix, values, precision=lax.Precision.HIGHEST)  13.1 us
    ppermute x2, waiting for transfers between devices, from_partner(): return lax.ppermute(block, axis, route)  11.2 us
  transfers between devices with their start and end apart: 2, of which 2 were waited for; matrix products, arithmetic and copies ran while one was open for 1% of the time, Pallas kernels for 0%

commit v1 on v0

v1 whole, which is shorter than its diff:
```python
import functools

import jax
import jax.numpy as jnp
from jax import lax
from jax.experimental import pallas as pl
from jax.experimental.pallas import tpu as pltpu
from jax.sharding import PartitionSpec as P

MESH = pl.DeviceIdType.MESH
F32 = jnp.float32
BF16 = jnp.bfloat16
NN = (((1,), (0,)), ((), ()))
NT = (((1,), (1,)), ((), ()))


def split(x):
    high = x.astype(BF16)
    return high, (x - high.astype(F32)).astype(BF16)


def product(left, right, dims):
    dot = functools.partial(lax.dot_general, dimension_numbers=dims, preferred_element_type=F32)
    return dot(left[0], right[0]) + (dot(left[0], right[1]) + dot(left[1], right[0]))


def complex_product(left, right, dims):
    real = product(left[0], right[0], dims) - product(left[1], right[1], dims)
    imag = product(left[0], right[1], dims) + product(left[1], right[0], dims)
    return real, imag


def top_rows(shape):
    return lax.broadcasted_iota(jnp.int32, shape, 1) < 4


def interleave(real, imag):
    a = real.reshape(-1, 8, real.shape[-1])
    b = imag.reshape(-1, 8, imag.shape[-1])
    top = top_rows(a.shape)
    even = jnp.where(top, a, pltpu.roll(b, 4, 1))
    odd = jnp.where(top, pltpu.roll(a, 4, 1), b)
    return jnp.stack([even, odd], axis=1).reshape(-1, real.shape[-1])


def deinterleave(both):
    pairs = both.reshape(-1, 2, 8, both.shape[-1])
    even, odd = pairs[:, 0], pairs[:, 1]
    top = top_rows(even.shape)
    real = jnp.where(top, even, pltpu.roll(odd, 4, 1))
    imag = jnp.where(top, pltpu.roll(even, 4, 1), odd)
    return real.reshape(-1, both.shape[-1]), imag.reshape(-1, both.shape[-1])


def kernel(n_narrow, n_wide, x_hbm, g1_hbm, g2_hbm, gs_hbm, out_hbm,
           x, gates, split_gates, send_a, state_a, send_b, state_b, turned0, got0,
           turned1, got1, tsend_a, tstate_a, tsend_b, tstate_b, result,
           in_sem, out_sem, swap_send, swap_recv, group_send, group_recv):
    n = lax.axis_index("narrow")
    w = lax.axis_index("wide")
    reg = x.shape[-1]
    half = reg // 2
    top_bit = n_narrow.bit_length() - 2
    bits = (lax.rem(n, 2), lax.rem(n // 2**top_bit, 2))
    partners = (n + 1 - 2 * bits[0], n + (1 - 2 * bits[1]) * 2**top_bit)

    loads = [
        pltpu.make_async_copy(g1_hbm, gates.at[0], in_sem.at[0]),
        pltpu.make_async_copy(x_hbm.at[:, 0], x.at[:, 0], in_sem.at[1]),
        pltpu.make_async_copy(g2_hbm, gates.at[1], in_sem.at[2]),
        pltpu.make_async_copy(x_hbm.at[:, 1], x.at[:, 1], in_sem.at[3]),
        pltpu.make_async_copy(gs_hbm.at[0], gates.at[2], in_sem.at[4]),
        pltpu.make_async_copy(gs_hbm.at[1], gates.at[3], in_sem.at[5]),
    ]
    for load in loads:
        load.start()

    barrier = pltpu.get_barrier_semaphore()
    for partner in partners:
        pl.semaphore_signal(barrier, inc=1, device_id=(partner, w), device_id_type=MESH)

    @pl.loop(1, n_wide)
    def _(k):
        pl.semaphore_signal(barrier, inc=1, device_id=(n, lax.rem(w + k, n_wide)), device_id_type=MESH)

    def prepare(index):
        for part in range(2):
            split_gates[index, part, 0], split_gates[index, part, 1] = split(gates[index, part])

    def gate(index, rows=slice(None)):
        return [(split_gates[index, part, 0, rows, :], split_gates[index, part, 1, rows, :]) for part in range(2)]

    def swap(number, slot, source, target):
        return pltpu.make_async_remote_copy(
            src_ref=source, dst_ref=target, send_sem=swap_send.at[slot], recv_sem=swap_recv.at[slot],
            device_id=(partners[number], w), device_id_type=MESH)

    def group(slot, source, target):
        @pl.loop(1, n_wide)
        def _(k):
            other = lax.rem(w + k, n_wide)
            pltpu.make_async_remote_copy(
                src_ref=source.at[pl.ds(pl.multiple_of(other * 8, 8), 8)],
                dst_ref=target.at[pl.ds(pl.multiple_of(w * 8, 8), 8)],
                send_sem=group_send.at[slot], recv_sem=group_recv.at[slot],
                device_id=(n, other), device_id_type=MESH).start()
        own = pl.ds(pl.multiple_of(w * 8, 8), 8)
        target[own, :] = source[own, :]

    def group_wait(slot, source, target):
        moved = pl.ds(0, 8 * (n_wide - 1))
        whole = pltpu.make_async_remote_copy(
            src_ref=source.at[moved], dst_ref=target.at[moved],
            send_sem=group_send.at[slot], recv_sem=group_recv.at[slot],
            device_id=(n, lax.rem(w + 1, n_wide)), device_id_type=MESH)
        return whole

    def rows_of(bit):
        return pl.ds(pl.multiple_of(bit * half, half), half)

    def natural_gate(index, number, values, send, state):
        bit = bits[number]
        send[0], send[1] = complex_product(gate(index, rows_of(1 - bit)), values, NN)
        copy = swap(number, number, send, state.at[:, rows_of(bit), :])
        keep = functools.partial(keep_natural, index, bit, values, state)
        return copy, keep

    def keep_natural(index, bit, values, state):
        real, imag = complex_product(gate(index, rows_of(bit)), values, NN)
        state[0, rows_of(bit), :] = real
        state[1, rows_of(bit), :] = imag

    def turned_gate(index, number, values, send, state):
        bit = bits[number]
        send[0], send[1] = complex_product(values, gate(index, rows_of(1 - bit)), NT)
        copy = swap(number, 2 + number, send, state.at[bit])
        keep = functools.partial(keep_turned, index, bit, values, state)
        return copy, keep

    def keep_turned(index, bit, values, state):
        real, imag = complex_product(values, gate(index, rows_of(bit)), NT)
        state[bit, 0] = real
        state[bit, 1] = imag

    def both_halves(state):
        return [split(jnp.concatenate([state[0, part], state[1, part]], axis=-1)) for part in range(2)]

    def pair(ref):
        return [split(ref[0]), split(ref[1])]

    loads[0].wait()
    prepare(0)
    loads[1].wait()
    values = [split(x[0, 0]), split(x[1, 0])]
    swap0, keep = natural_gate(0, 0, values, send_a, state_a)
    keep()
    loads[2].wait()
    prepare(1)
    loads[3].wait()
    values = [split(x[0, 1]), split(x[1, 1])]
    turned1[...] = interleave(*complex_product(gate(1), values, NT))

    pl.semaphore_wait(barrier, n_wide - 1 + len(partners))
    swap0.start()
    group(1, turned1, got1)

    loads[4].wait()
    prepare(2)
    loads[5].wait()
    prepare(3)

    swap0.wait_recv()
    swap1, keep = natural_gate(2, 1, pair(state_a), send_b, state_b)
    swap1.start()
    keep()
    swap1.wait_recv()
    turned0[...] = interleave(*complex_product(gate(1), pair(state_b), NT))
    group(0, turned0, got0)

    moved1 = group_wait(1, turned1, got1)
    moved1.wait_recv()
    values = [split(part) for part in deinterleave(got1[...])]
    swap2, keep = turned_gate(0, 0, values, tsend_a, tstate_a)
    swap2.start()
    keep()
    swap2.wait_recv()
    swap3, keep = turned_gate(2, 1, both_halves(tstate_a), tsend_b, tstate_b)
    swap3.start()
    keep()
    swap3.wait_recv()
    result[0, 1], result[1, 1] = complex_product(gate(3), both_halves(tstate_b), NT)
    store1 = pltpu.make_async_copy(result.at[:, 1], out_hbm.at[:, 1], out_sem.at[1])
    store1.start()

    moved0 = group_wait(0, turned0, got0)
    moved0.wait_recv()
    values = [split(part) for part in deinterleave(got0[...])]
    result[0, 0], result[1, 0] = complex_product(gate(3), values, NT)
    store0 = pltpu.make_async_copy(result.at[:, 0], out_hbm.at[:, 0], out_sem.at[0])
    store0.start()

    for copy in (swap0, swap1, swap2, swap3, moved1, moved0):
        copy.wait_send()
    store1.wait()
    store0.wait()


def solution(mesh):
    n_narrow, n_wide = mesh.shape["narrow"], mesh.shape["wide"]

    def shards(amplitudes, first_gate, second_gate, swap_gates):
        block = amplitudes.shape[2:]
        reg = block[-1]
        half = reg // 2
        vmem = lambda *shape: pltpu.VMEM(shape, F32)
        out = pl.pallas_call(
            functools.partial(kernel, n_narrow, n_wide),
            out_shape=jax.ShapeDtypeStruct(block, F32),
            in_specs=[pl.BlockSpec(memory_space=pl.ANY)] * 4,
            out_specs=pl.BlockSpec(memory_space=pl.ANY),
            scratch_shapes=[
                vmem(*block),
                vmem(4, 2, reg, reg),
                pltpu.VMEM((4, 2, 2, reg, reg), BF16),
                vmem(2, half, reg),
                vmem(2, reg, reg),
                vmem(2, half, reg),
                vmem(2, reg, reg),
                vmem(2 * reg, reg),
                vmem(2 * reg, reg),
                vmem(2 * reg, reg),
                vmem(2 * reg, reg),
                vmem(2, reg, half),
                vmem(2, 2, reg, half),
                vmem(2, reg, half),
                vmem(2, 2, reg, half),
                vmem(*block),
                pltpu.SemaphoreType.DMA((6,)),
                pltpu.SemaphoreType.DMA((2,)),
                pltpu.SemaphoreType.DMA((4,)),
                pltpu.SemaphoreType.DMA((4,)),
                pltpu.SemaphoreType.DMA((2,)),
                pltpu.SemaphoreType.DMA((2,)),
            ],
            compiler_params=pltpu.CompilerParams(
                collective_id=0, has_side_effects=True, vmem_limit_bytes=40 * 2**20),
            cost_estimate=pl.CostEstimate(flops=8 * 2**30 // 2, bytes_accessed=4 * 2**20, transcendentals=0),
        )(amplitudes[0, 0], first_gate, second_gate, swap_gates)
        return out[None, None]

    return jax.shard_map(
        shards,
        mesh=mesh,
        in_specs=(P("narrow", "wide", None, None, None, None), P(), P(), P()),
        out_specs=P("narrow", "wide", None, None, None, None),
        check_vma=False,
    )
```

time: 132 us -> 81.1 us (0.61)
  the two profiles are of different devices: /device:TPU:1 before, /device:TPU:41 now
where the time goes in v1:
time: 81.1 us; the launch traced here: 80.8 us
  Pallas kernels  75.2 us (93%)
  local copies, waits for them, and re-layouts  5.5 us (7%)
    pallas_call x1, Pallas kernels, shards(): pl.pallas_call(functools.partial(kernel, n_narrow, n_wide), out_shape=jax...  75.2 us
    unnamed x9, local copies, waits for them, and re-layouts  5.5 us

profile of v1, /device:TPU:41, one launch (start us, length us, event | category | flops | bytes accessed | tf_op | source)
XLA Modules:
  0.0 80.8 jit_solution(6849235071505522883)
XLA Ops:
  0.0 0.0 copy-start
  0.0 1.2 %copy-done = f32[1,1,2,2,256,256]{5,4,3,2,1,0:T(8,128)S(1)} copy-done((f32[1,1,2,2,256,256]{5,4,3,2,1,0:T(8,128)S(1)}, f32[1,1,2,2,256,256]{5,4,3,2,1,0:T(8,128)}, u32[]{:S(2)}) %copy-start) | copy-done | bytes 1048600
  1.2 0.0 copy-start.1
  1.2 1.2 %copy-done.1 = f32[2,2,256,256]{3,2,1,0:T(8,128)S(1)} copy-done((f32[2,2,256,256]{3,2,1,0:T(8,128)S(1)}, f32[2,2,256,256]{3,2,1,0:T(8,128)}, u32[]{:S(2)}) %copy-start.1) | copy-done | bytes 1048600
  2.5 0.0 copy-start.2
  2.5 1.0 %copy-done.2 = f32[2,256,256]{2,1,0:T(8,128)S(1)} copy-done((f32[2,256,256]{2,1,0:T(8,128)S(1)}, f32[2,256,256]{2,1,0:T(8,128)}, u32[]{:S(2)}) %copy-start.2) | copy-done | bytes 524312
  3.5 0.0 copy-start.3
  3.5 1.0 %copy-done.3 = f32[2,256,256]{2,1,0:T(8,128)S(1)} copy-done((f32[2,256,256]{2,1,0:T(8,128)S(1)}, f32[2,256,256]{2,1,0:T(8,128)}, u32[]{:S(2)}) %copy-start.3) | copy-done | bytes 524312
  4.5 75.2 %shard_map.46 = f32[2,2,256,256]{3,2,1,0:T(8,128)S(1)} custom-call(f32[2,2,256,256]{3,2,1,0:T(8,128)S(1)} %bitcast.3, f32[2,256,256]{2,1,0:T(8,128)S(1)} %copy-done.2, f32[2,256,256]{2,1,0:T(8,128)S(1)} %copy-done.3, f32[2,2,256,256]{3,2,1,0:T(8,128)S(1)} %copy-done.1), custom_call_target="tpu_custom_call" | custom-call | flops 4294967296 | bytes 4194304 | tf_op jit(solution)/shard_map/pallas_call | solution.py:216
  79.8 1.0 %copy.6 = f32[1,1,2,2,256,256]{5,4,3,2,1,0:T(8,128)} copy(f32[1,1,2,2,256,256]{5,4,3,2,1,0:T(8,128)S(1)} %bitcast.2) | data formatting | bytes 2097152
Async XLA Ops:
  0.0 1.2 %copy-start = (f32[1,1,2,2,256,256]{5,4,3,2,1,0:T(8,128)S(1)}, f32[1,1,2,2,256,256]{5,4,3,2,1,0:T(8,128)}, u32[]{:S(2)}) copy-start(f32[1,1,2,2,256,256]{5,4,3,2,1,0:T(8,128)} %param.4) | copy-start | bytes 3145732
  1.2 1.2 %copy-start.1 = (f32[2,2,256,256]{3,2,1,0:T(8,128)S(1)}, f32[2,2,256,256]{3,2,1,0:T(8,128)}, u32[]{:S(2)}) copy-start(f32[2,2,256,256]{3,2,1,0:T(8,128)} %gs_hbm.1) | copy-start | bytes 3145732
  2.5 1.0 %copy-start.2 = (f32[2,256,256]{2,1,0:T(8,128)S(1)}, f32[2,256,256]{2,1,0:T(8,128)}, u32[]{:S(2)}) copy-start(f32[2,256,256]{2,1,0:T(8,128)} %g1_hbm.1) | copy-start | bytes 1572868
  3.5 1.0 %copy-start.3 = (f32[2,256,256]{2,1,0:T(8,128)S(1)}, f32[2,256,256]{2,1,0:T(8,128)}, u32[]{:S(2)}) copy-start(f32[2,256,256]{2,1,0:T(8,128)} %g2_hbm.1) | copy-start | bytes 1572868

commit v2 on v1

--- a/solution.py
+++ b/solution.py
@@ -10,6 +10,8 @@
 MESH = pl.DeviceIdType.MESH
 F32 = jnp.float32
 BF16 = jnp.bfloat16
+PARTS = (4, 4)
+PIECES = 2
 NN = (((1,), (0,)), ((), ()))
 NT = (((1,), (1,)), ((), ()))
 
@@ -96,14 +98,19 @@
             device_id=(partners[number], w), device_id_type=MESH)
 
     def group(slot, source, target):
-        @pl.loop(1, n_wide)
+        size = n_wide // PARTS[slot]
+
+        @pl.loop(0, n_wide)
         def _(k):
-            other = lax.rem(w + k, n_wide)
-            pltpu.make_async_remote_copy(
-                src_ref=source.at[pl.ds(pl.multiple_of(other * 8, 8), 8)],
-                dst_ref=target.at[pl.ds(pl.multiple_of(w * 8, 8), 8)],
-                send_sem=group_send.at[slot], recv_sem=group_recv.at[slot],
-                device_id=(n, other), device_id_type=MESH).start()
+            other = k // size * size + lax.rem(w + k, size)
+
+            @pl.when(other != w)
+            def _():
+                pltpu.make_async_remote_copy(
+                    src_ref=source.at[pl.ds(pl.multiple_of(other * 8, 8), 8)],
+                    dst_ref=target.at[pl.ds(pl.multiple_of(w * 8, 8), 8)],
+                    send_sem=group_send.at[slot], recv_sem=group_recv.at[slot],
+                    device_id=(n, other), device_id_type=MESH).start()
         own = pl.ds(pl.multiple_of(w * 8, 8), 8)
         target[own, :] = source[own, :]
 
@@ -130,20 +137,18 @@
         state[0, rows_of(bit), :] = real
         state[1, rows_of(bit), :] = imag
 
-    def turned_gate(index, number, values, send, state):
+    def turned_gate(index, number, piece, values, send, state):
         bit = bits[number]
-        send[0], send[1] = complex_product(values, gate(index, rows_of(1 - bit)), NT)
-        copy = swap(number, 2 + number, send, state.at[bit])
-        keep = functools.partial(keep_turned, index, bit, values, state)
-        return copy, keep
-
-    def keep_turned(index, bit, values, state):
+        send[piece, 0], send[piece, 1] = complex_product(values, gate(index, rows_of(1 - bit)), NT)
+        copy = swap(number, 2 + 2 * piece + number, send.at[piece], state.at[piece, bit])
+        copy.start()
         real, imag = complex_product(values, gate(index, rows_of(bit)), NT)
-        state[bit, 0] = real
-        state[bit, 1] = imag
-
-    def both_halves(state):
-        return [split(jnp.concatenate([state[0, part], state[1, part]], axis=-1)) for part in range(2)]
+        state[piece, bit, 0] = real
+        state[piece, bit, 1] = imag
+        return copy
+
+    def both_halves(state, piece):
+        return [split(jnp.concatenate([state[piece, 0, part], state[piece, 1, part]], axis=-1)) for part in range(2)]
 
     def pair(ref):
         return [split(ref[0]), split(ref[1])]
@@ -179,16 +184,17 @@
 
     moved1 = group_wait(1, turned1, got1)
     moved1.wait_recv()
-    values = [split(part) for part in deinterleave(got1[...])]
-    swap2, keep = turned_gate(0, 0, values, tsend_a, tstate_a)
-    swap2.start()
-    keep()
-    swap2.wait_recv()
-    swap3, keep = turned_gate(2, 1, both_halves(tstate_a), tsend_b, tstate_b)
-    swap3.start()
-    keep()
-    swap3.wait_recv()
-    result[0, 1], result[1, 1] = complex_product(gate(3), both_halves(tstate_b), NT)
+    swaps2, swaps3 = [], []
+    for piece in range(PIECES):
+        values = [split(part) for part in deinterleave(got1[piece * reg:(piece + 1) * reg, :])]
+        swaps2.append(turned_gate(0, 0, piece, values, tsend_a, tstate_a))
+    for piece in range(PIECES):
+        swaps2[piece].wait_recv()
+        swaps3.append(turned_gate(2, 1, piece, both_halves(tstate_a, piece), tsend_b, tstate_b))
+    for piece in range(PIECES):
+        swaps3[piece].wait_recv()
+        columns = slice(piece * half, (piece + 1) * half)
+        result[0, 1, :, columns], result[1, 1, :, columns] = complex_product(gate(3), both_halves(tstate_b, piece), NT)
     store1 = pltpu.make_async_copy(result.at[:, 1], out_hbm.at[:, 1], out_sem.at[1])
     store1.start()
 
@@ -199,7 +205,7 @@
     store0 = pltpu.make_async_copy(result.at[:, 0], out_hbm.at[:, 0], out_sem.at[0])
     store0.start()
 
-    for copy in (swap0, swap1, swap2, swap3, moved1, moved0):
+    for copy in (swap0, swap1, *swaps2, *swaps3, moved1, moved0):
         copy.wait_send()
     store1.wait()
     store0.wait()
@@ -230,20 +236,20 @@
                 vmem(2 * reg, reg),
                 vmem(2 * reg, reg),
                 vmem(2 * reg, reg),
-                vmem(2, reg, half),
-                vmem(2, 2, reg, half),
-                vmem(2, reg, half),
-                vmem(2, 2, reg, half),
+                vmem(PIECES, 2, reg // PIECES, half),
+                vmem(PIECES, 2, 2, reg // PIECES, half),
+                vmem(PIECES, 2, reg // PIECES, half),
+                vmem(PIECES, 2, 2, reg // PIECES, half),
                 vmem(*block),
                 pltpu.SemaphoreType.DMA((6,)),
                 pltpu.SemaphoreType.DMA((2,)),
-                pltpu.SemaphoreType.DMA((4,)),
-                pltpu.SemaphoreType.DMA((4,)),
+                pltpu.SemaphoreType.DMA((2 + 2 * PIECES,)),
+                pltpu.SemaphoreType.DMA((2 + 2 * PIECES,)),
                 pltpu.SemaphoreType.DMA((2,)),
                 pltpu.SemaphoreType.DMA((2,)),
             ],
             compiler_params=pltpu.CompilerParams(
-                collective_id=0, has_side_effects=True, vmem_limit_bytes=40 * 2**20),
+                collective_id=0, has_side_effects=True, vmem_limit_bytes=60 * 2**20),
             cost_estimate=pl.CostEstimate(flops=8 * 2**30 // 2, bytes_accessed=4 * 2**20, transcendentals=0),
         )(amplitudes[0, 0], first_gate, second_gate, swap_gates)
         return out[None, None]

time: 81.1 us -> 76.3 us (0.941)
  the two profiles are of different devices: /device:TPU:41 before, /device:TPU:2 now
where the time goes in v2:
time: 76.3 us; the launch traced here: 76.1 us
  Pallas kernels  73.8 us (97%)
  local copies, waits for them, and re-layouts  2.29 us (3%)
    pallas_call x1, Pallas kernels, shards(): pl.pallas_call(functools.partial(kernel, n_narrow, n_wide), out_shape=jax...  73.8 us
    unnamed x1, local copies, waits for them, and re-layouts  2.29 us

profile of v2, /device:TPU:2, one launch (start us, length us, event | category | flops | bytes accessed | tf_op | source)
XLA Modules:
  0.0 76.1 jit_solution(7393009306450165752)
XLA Ops:
  0.0 73.8 %shard_map.46 = f32[2,2,256,256]{3,2,1,0:T(8,128)} custom-call(f32[2,2,256,256]{3,2,1,0:T(8,128)} %bitcast.3, f32[2,256,256]{2,1,0:T(8,128)} %g1_hbm.1, f32[2,256,256]{2,1,0:T(8,128)} %g2_hbm.1, f32[2,2,256,256]{3,2,1,0:T(8,128)} %gs_hbm.1), custom_call_target="tpu_custom_call" | custom-call | flops 4294967296 | bytes 4194304 | tf_op jit(solution)/shard_map/pallas_call | solution.py:222
  73.8 2.3 %copy.6 = f32[1,1,2,2,256,256]{5,4,3,2,1,0:T(8,128)} copy(f32[1,1,2,2,256,256]{5,4,3,2,1,0:T(8,128)} %bitcast.2) | data formatting | bytes 2097152

commit v3 on v2

--- a/solution.py
+++ b/solution.py
@@ -10,7 +10,7 @@
 MESH = pl.DeviceIdType.MESH
 F32 = jnp.float32
 BF16 = jnp.bfloat16
-PARTS = (4, 4)
+ORDER = ((0, 0), (1, 0), (0, 1), (2, 0), (1, 1), (3, 0), (2, 1), (3, 1))
 PIECES = 2
 NN = (((1,), (0,)), ((), ()))
 NT = (((1,), (1,)), ((), ()))
@@ -98,19 +98,21 @@
             device_id=(partners[number], w), device_id_type=MESH)
 
     def group(slot, source, target):
-        size = n_wide // PARTS[slot]
-
-        @pl.loop(0, n_wide)
-        def _(k):
-            other = k // size * size + lax.rem(w + k, size)
-
-            @pl.when(other != w)
-            def _():
-                pltpu.make_async_remote_copy(
-                    src_ref=source.at[pl.ds(pl.multiple_of(other * 8, 8), 8)],
-                    dst_ref=target.at[pl.ds(pl.multiple_of(w * 8, 8), 8)],
-                    send_sem=group_send.at[slot], recv_sem=group_recv.at[slot],
-                    device_id=(n, other), device_id_type=MESH).start()
+        run = n_wide // 8
+
+        for quarter, middle in ORDER:
+            @pl.loop(0, run)
+            def _(k):
+                place = lax.rem(w // 4 * 2 + lax.rem(w, 2) + k, run)
+                other = quarter * 2 * run + place // 2 * 4 + middle * 2 + lax.rem(place, 2)
+
+                @pl.when(other != w)
+                def _():
+                    pltpu.make_async_remote_copy(
+                        src_ref=source.at[pl.ds(pl.multiple_of(other * 8, 8), 8)],
+                        dst_ref=target.at[pl.ds(pl.multiple_of(w * 8, 8), 8)],
+                        send_sem=group_send.at[slot], recv_sem=group_recv.at[slot],
+                        device_id=(n, other), device_id_type=MESH).start()
         own = pl.ds(pl.multiple_of(w * 8, 8), 8)
         target[own, :] = source[own, :]
 
@@ -125,22 +127,21 @@
     def rows_of(bit):
         return pl.ds(pl.multiple_of(bit * half, half), half)
 
-    def natural_gate(index, number, values, send, state):
+    def natural_gate(index, number, piece, values, send, state):
         bit = bits[number]
-        send[0], send[1] = complex_product(gate(index, rows_of(1 - bit)), values, NN)
-        copy = swap(number, number, send, state.at[:, rows_of(bit), :])
-        keep = functools.partial(keep_natural, index, bit, values, state)
-        return copy, keep
-
-    def keep_natural(index, bit, values, state):
+        send[piece, 0], send[piece, 1] = complex_product(gate(index, rows_of(1 - bit)), values, NN)
+        copy = swap(number, 2 * piece + number, send.at[piece], state.at[piece, :, rows_of(bit), :])
+        return copy, functools.partial(keep_natural, index, bit, piece, values, state)
+
+    def keep_natural(index, bit, piece, values, state):
         real, imag = complex_product(gate(index, rows_of(bit)), values, NN)
-        state[0, rows_of(bit), :] = real
-        state[1, rows_of(bit), :] = imag
+        state[piece, 0, rows_of(bit), :] = real
+        state[piece, 1, rows_of(bit), :] = imag
 
     def turned_gate(index, number, piece, values, send, state):
         bit = bits[number]
         send[piece, 0], send[piece, 1] = complex_product(values, gate(index, rows_of(1 - bit)), NT)
-        copy = swap(number, 2 + 2 * piece + number, send.at[piece], state.at[piece, bit])
+        copy = swap(number, 2 * PIECES + 2 * piece + number, send.at[piece], state.at[piece, bit])
         copy.start()
         real, imag = complex_product(values, gate(index, rows_of(bit)), NT)
         state[piece, bit, 0] = real
@@ -150,15 +151,18 @@
     def both_halves(state, piece):
         return [split(jnp.concatenate([state[piece, 0, part], state[piece, 1, part]], axis=-1)) for part in range(2)]
 
-    def pair(ref):
-        return [split(ref[0]), split(ref[1])]
+    def columns(piece):
+        return slice(piece * reg // PIECES, (piece + 1) * reg // PIECES)
 
     loads[0].wait()
     prepare(0)
     loads[1].wait()
-    values = [split(x[0, 0]), split(x[1, 0])]
-    swap0, keep = natural_gate(0, 0, values, send_a, state_a)
-    keep()
+    swaps0, swaps1 = [], []
+    for piece in range(PIECES):
+        values = [split(x[part, 0, :, columns(piece)]) for part in range(2)]
+        copy, keep = natural_gate(0, 0, piece, values, send_a, state_a)
+        keep()
+        swaps0.append(copy)
     loads[2].wait()
     prepare(1)
     loads[3].wait()
@@ -166,7 +170,8 @@
     turned1[...] = interleave(*complex_product(gate(1), values, NT))
 
     pl.semaphore_wait(barrier, n_wide - 1 + len(partners))
-    swap0.start()
+    for copy in swaps0:
+        copy.start()
     group(1, turned1, got1)
 
     loads[4].wait()
@@ -174,12 +179,17 @@
     loads[5].wait()
     prepare(3)
 
-    swap0.wait_recv()
-    swap1, keep = natural_gate(2, 1, pair(state_a), send_b, state_b)
-    swap1.start()
-    keep()
-    swap1.wait_recv()
-    turned0[...] = interleave(*complex_product(gate(1), pair(state_b), NT))
+    for piece in range(PIECES):
+        swaps0[piece].wait_recv()
+        values = [split(state_a[piece, part]) for part in range(2)]
+        copy, keep = natural_gate(2, 1, piece, values, send_b, state_b)
+        copy.start()
+        keep()
+        swaps1.append(copy)
+    for copy in swaps1:
+        copy.wait_recv()
+    values = [split(jnp.concatenate([state_b[piece, part] for piece in range(PIECES)], axis=-1)) for part in range(2)]
+    turned0[...] = interleave(*complex_product(gate(1), values, NT))
     group(0, turned0, got0)
 
     moved1 = group_wait(1, turned1, got1)
@@ -193,8 +203,7 @@
         swaps3.append(turned_gate(2, 1, piece, both_halves(tstate_a, piece), tsend_b, tstate_b))
     for piece in range(PIECES):
         swaps3[piece].wait_recv()
-        columns = slice(piece * half, (piece + 1) * half)
-        result[0, 1, :, columns], result[1, 1, :, columns] = complex_product(gate(3), both_halves(tstate_b, piece), NT)
+        result[0, 1, :, columns(piece)], result[1, 1, :, columns(piece)] = complex_product(gate(3), both_halves(tstate_b, piece), NT)
     store1 = pltpu.make_async_copy(result.at[:, 1], out_hbm.at[:, 1], out_sem.at[1])
     store1.start()
 
@@ -205,7 +214,7 @@
     store0 = pltpu.make_async_copy(result.at[:, 0], out_hbm.at[:, 0], out_sem.at[0])
     store0.start()
 
-    for copy in (swap0, swap1, *swaps2, *swaps3, moved1, moved0):
+    for copy in (*swaps0, *swaps1, *swaps2, *swaps3, moved1, moved0):
         copy.wait_send()
     store1.wait()
     store0.wait()
@@ -228,10 +237,10 @@
                 vmem(*block),
                 vmem(4, 2, reg, reg),
                 pltpu.VMEM((4, 2, 2, reg, reg), BF16),
-                vmem(2, half, reg),
-                vmem(2, reg, reg),
-                vmem(2, half, reg),
-                vmem(2, reg, reg),
+                vmem(PIECES, 2, half, reg // PIECES),
+                vmem(PIECES, 2, reg, reg // PIECES),
+                vmem(PIECES, 2, half, reg // PIECES),
+                vmem(PIECES, 2, reg, reg // PIECES),
                 vmem(2 * reg, reg),
                 vmem(2 * reg, reg),
                 vmem(2 * reg, reg),
@@ -243,8 +252,8 @@
                 vmem(*block),
                 pltpu.SemaphoreType.DMA((6,)),
                 pltpu.SemaphoreType.DMA((2,)),
-                pltpu.SemaphoreType.DMA((2 + 2 * PIECES,)),
-                pltpu.SemaphoreType.DMA((2 + 2 * PIECES,)),
+                pltpu.SemaphoreType.DMA((4 * PIECES,)),
+                pltpu.SemaphoreType.DMA((4 * PIECES,)),
                 pltpu.SemaphoreType.DMA((2,)),
                 pltpu.SemaphoreType.DMA((2,)),
             ],

time: 76.3 us -> 74 us (0.970)
  the two profiles are of different devices: /device:TPU:2 before, /device:TPU:41 now
where the time goes in v3:
time: 74 us; the launch traced here: 73.8 us
  Pallas kernels  71.5 us (97%)
  local copies, waits for them, and re-layouts  2.29 us (3%)
    pallas_call x1, Pallas kernels, shards(): pl.pallas_call(functools.partial(kernel, n_narrow, n_wide), out_shape=jax...  71.5 us
    unnamed x1, local copies, waits for them, and re-layouts  2.29 us

profile of v3, /device:TPU:41, one launch (start us, length us, event | category | flops | bytes accessed | tf_op | source)
XLA Modules:
  0.0 73.8 jit_solution(9972997976328406585)
XLA Ops:
  0.0 71.5 %shard_map.46 = f32[2,2,256,256]{3,2,1,0:T(8,128)} custom-call(f32[2,2,256,256]{3,2,1,0:T(8,128)} %bitcast.3, f32[2,256,256]{2,1,0:T(8,128)} %g1_hbm.1, f32[2,256,256]{2,1,0:T(8,128)} %g2_hbm.1, f32[2,2,256,256]{3,2,1,0:T(8,128)} %gs_hbm.1), custom_call_target="tpu_custom_call" | custom-call | flops 4294967296 | bytes 4194304 | tf_op jit(solution)/shard_map/pallas_call | solution.py:231
  71.5 2.3 %copy.6 = f32[1,1,2,2,256,256]{5,4,3,2,1,0:T(8,128)} copy(f32[1,1,2,2,256,256]{5,4,3,2,1,0:T(8,128)} %bitcast.2) | data formatting | bytes 2097152

commit v4 on v3

--- a/solution.py
+++ b/solution.py
@@ -12,6 +12,7 @@
 BF16 = jnp.bfloat16
 ORDER = ((0, 0), (1, 0), (0, 1), (2, 0), (1, 1), (3, 0), (2, 1), (3, 1))
 PIECES = 2
+FINER = 4
 NN = (((1,), (0,)), ((), ()))
 NT = (((1,), (1,)), ((), ()))
 
@@ -148,8 +149,9 @@
         state[piece, bit, 1] = imag
         return copy
 
-    def both_halves(state, piece):
-        return [split(jnp.concatenate([state[piece, 0, part], state[piece, 1, part]], axis=-1)) for part in range(2)]
+    def both_halves(state, pieces):
+        rows = [[jnp.concatenate([state[piece, 0, part], state[piece, 1, part]], axis=-1) for piece in pieces] for part in range(2)]
+        return [split(jnp.concatenate(of_part, axis=0)) for of_part in rows]
 
     def columns(piece):
         return slice(piece * reg // PIECES, (piece + 1) * reg // PIECES)
@@ -195,15 +197,18 @@
     moved1 = group_wait(1, turned1, got1)
     moved1.wait_recv()
     swaps2, swaps3 = [], []
+    tall = 2 * reg // FINER
+    for piece in range(FINER):
+        values = [split(part) for part in deinterleave(got1[piece * tall:(piece + 1) * tall, :])]
+        swaps2.append(turned_gate(0, 0, piece, values, tsend_a, tstate_a))
+    for piece in range(FINER):
+        swaps2[piece].wait_recv()
+        swaps3.append(turned_gate(2, 1, piece, both_halves(tstate_a, [piece]), tsend_b, tstate_b))
     for piece in range(PIECES):
-        values = [split(part) for part in deinterleave(got1[piece * reg:(piece + 1) * reg, :])]
-        swaps2.append(turned_gate(0, 0, piece, values, tsend_a, tstate_a))
-    for piece in range(PIECES):
-        swaps2[piece].wait_recv()
-        swaps3.append(turned_gate(2, 1, piece, both_halves(tstate_a, piece), tsend_b, tstate_b))
-    for piece in range(PIECES):
-        swaps3[piece].wait_recv()
-        result[0, 1, :, columns(piece)], result[1, 1, :, columns(piece)] = complex_product(gate(3), both_halves(tstate_b, piece), NT)
+        parts = range(piece * FINER // PIECES, (piece + 1) * FINER // PIECES)
+        for part in parts:
+            swaps3[part].wait_recv()
+        result[0, 1, :, columns(piece)], result[1, 1, :, columns(piece)] = complex_product(gate(3), both_halves(tstate_b, parts), NT)
     store1 = pltpu.make_async_copy(result.at[:, 1], out_hbm.at[:, 1], out_sem.at[1])
     store1.start()
 
@@ -245,15 +250,15 @@
                 vmem(2 * reg, reg),
                 vmem(2 * reg, reg),
                 vmem(2 * reg, reg),
-                vmem(PIECES, 2, reg // PIECES, half),
-                vmem(PIECES, 2, 2, reg // PIECES, half),
-                vmem(PIECES, 2, reg // PIECES, half),
-                vmem(PIECES, 2, 2, reg // PIECES, half),
+                vmem(FINER, 2, reg // FINER, half),
+                vmem(FINER, 2, 2, reg // FINER, half),
+                vmem(FINER, 2, reg // FINER, half),
+                vmem(FINER, 2, 2, reg // FINER, half),
                 vmem(*block),
                 pltpu.SemaphoreType.DMA((6,)),
                 pltpu.SemaphoreType.DMA((2,)),
-                pltpu.SemaphoreType.DMA((4 * PIECES,)),
-                pltpu.SemaphoreType.DMA((4 * PIECES,)),
+                pltpu.SemaphoreType.DMA((2 * PIECES + 2 * FINER,)),
+                pltpu.SemaphoreType.DMA((2 * PIECES + 2 * FINER,)),
                 pltpu.SemaphoreType.DMA((2,)),
                 pltpu.SemaphoreType.DMA((2,)),
             ],

time: 74 us -> 74 us (level)
  no operation moved by 1% of the time
where the time goes in v4:
time: 74 us; the launch traced here: 73.9 us
  Pallas kernels  71.6 us (97%)
  local copies, waits for them, and re-layouts  2.29 us (3%)
    pallas_call x1, Pallas kernels, shards(): pl.pallas_call(functools.partial(kernel, n_narrow, n_wide), out_shape=jax...  71.6 us
    unnamed x1, local copies, waits for them, and re-layouts  2.29 us

profile of v4, /device:TPU:41, one launch (start us, length us, event | category | flops | bytes accessed | tf_op | source)
XLA Modules:
  0.0 73.9 jit_solution(6858637447038915104)
XLA Ops:
  0.0 71.6 %shard_map.46 = f32[2,2,256,256]{3,2,1,0:T(8,128)} custom-call(f32[2,2,256,256]{3,2,1,0:T(8,128)} %bitcast.3, f32[2,256,256]{2,1,0:T(8,128)} %g1_hbm.1, f32[2,256,256]{2,1,0:T(8,128)} %g2_hbm.1, f32[2,2,256,256]{3,2,1,0:T(8,128)} %gs_hbm.1), custom_call_target="tpu_custom_call" | custom-call | flops 4294967296 | bytes 4194304 | tf_op jit(solution)/shard_map/pallas_call | solution.py:236
  71.6 2.3 %copy.6 = f32[1,1,2,2,256,256]{5,4,3,2,1,0:T(8,128)} copy(f32[1,1,2,2,256,256]{5,4,3,2,1,0:T(8,128)} %bitcast.2) | data formatting | bytes 2097152
